TPU v7x, 32 devices: a whole 2x2x4 slice. The times are simulated.
32 devices in a mesh: groups: 2 (over y), hosts: 8 (over z, x), tensor: 2 (over core).
Axes of the slice: x: 2, y: 2, z: 4, core: 2. Of those that a mesh axis runs over, the one named last changes fastest.
Arguments:
- context_queries: bfloat16 [2048, 8192], P(('groups', 'hosts'), 'tensor'), parts along dimension 0, may hold values from -6 to 6
- context_keys: bfloat16 [2048, 1024], P(('groups', 'hosts'), 'tensor'), parts along dimension 0, may hold values from -6 to 6
- context_values: bfloat16 [2048, 1024], P(('groups', 'hosts'), 'tensor'), parts along dimension 0, may hold values from -6 to 6
- doc_ids: int32 [2048], P(('groups', 'hosts')), parts along dimension 0, may hold values from 0 to 31, never falling along the last dimension, each value on 1 to 128 neighbouring positions
- query_token_rows: bfloat16 [16, 8192], P(('groups', 'hosts'), 'tensor'), parts along dimension 0, may hold values from -6 to 6
- span_start: int32 [16], P(('groups', 'hosts')), parts along dimension 0, may hold values from 0 to 511
Outputs:
- block_out: bfloat16 [2048, 8192], P(('groups', 'hosts'), 'tensor'), parts along dimension 0
- answer: bfloat16 [16, 8192], P(('groups', 'hosts'), 'tensor'), parts along dimension 0
There are 2 independent parts, one for each index of `groups`. A program takes and returns all parts, laid end to end along the dimension named above; each array names one. Nothing has to cross between parts.
All inputs are finite; a program needn't handle non-finite values.
Results may differ from a plain program's by a relative error of at most 0.0043.
Values may be sent and summed in bfloat16 or wider, within the bound.
A program may use at most 64 MiB of HBM per device.

v0:
```python
import jax
import jax.numpy as jnp
from jax import lax
from jax.sharding import PartitionSpec as P

HEAD_SIZE = 128
MASKED_SCORE = -1e30


def from_root(value, axis, source):
    kept = jnp.where(lax.axis_index(axis) == source, value, 0).astype(value.dtype)
    return lax.psum(kept, axis)


def head_groups(matrix, kv_count):
    count_rows = matrix.shape[0]
    return matrix.reshape(
        count_rows, kv_count, matrix.shape[1] // (kv_count * HEAD_SIZE), HEAD_SIZE
    ).transpose(1, 0, 2, 3)


def kv_groups(matrix, kv_count):
    return matrix.reshape(matrix.shape[0], kv_count, HEAD_SIZE).transpose(1, 0, 2)


def block_attention(queries, key_rows, value_rows, visible, factor):
    kv_count = key_rows.shape[1] // HEAD_SIZE

    def block_per_head(operands):
        query_part, key_part, value_part = operands
        scores = (
            jnp.einsum("rgd,sd->rgs", query_part, key_part, preferred_element_type=jnp.float32)
            * factor
        )
        shown = visible[:, None, :]
        peak_score = jnp.max(jnp.where(shown, scores, MASKED_SCORE), -1, keepdims=True)
        weights = jnp.where(shown, jnp.exp(scores - peak_score), 0.0)
        totals = jnp.sum(weights, -1)
        output = jnp.einsum(
            "rgs,sd->rgd",
            weights.astype(jnp.bfloat16),
            value_part,
            preferred_element_type=jnp.float32,
        )
        return (output / totals[..., None]).astype(jnp.bfloat16)

    outputs = lax.map(
        block_per_head,
        (
            head_groups(queries, kv_count),
            kv_groups(key_rows, kv_count),
            kv_groups(value_rows, kv_count),
        ),
    )
    return outputs.transpose(1, 0, 2, 3).reshape(queries.shape[0], queries.shape[1])


def query_partials(queries, key_rows, value_rows, visible, factor):
    kv_count = key_rows.shape[1] // HEAD_SIZE

    def query_per_head(operands):
        query_part, key_part, value_part = operands
        scores = (
            jnp.einsum("qgd,sd->qgs", query_part, key_part, preferred_element_type=jnp.float32)
            * factor
        )
        shown = visible[:, None, :]
        peak_score = jnp.max(jnp.where(shown, scores, MASKED_SCORE), -1)
        weights = jnp.where(shown, jnp.exp(scores - peak_score[..., None]), 0.0)
        totals = jnp.sum(weights, -1)
        partial_acc = jnp.einsum(
            "qgs,sd->qgd",
            weights.astype(jnp.bfloat16),
            value_part,
            preferred_element_type=jnp.float32,
        )
        return (peak_score, totals, partial_acc)

    peaks, totals, accums = lax.map(
        query_per_head,
        (
            head_groups(queries, kv_count),
            kv_groups(key_rows, kv_count),
            kv_groups(value_rows, kv_count),
        ),
    )
    query_count = queries.shape[0]
    peaks = peaks.transpose(1, 0, 2).reshape(query_count, -1)
    totals = totals.transpose(1, 0, 2).reshape(query_count, -1)
    accums = accums.transpose(1, 0, 2, 3).reshape(query_count, -1)
    return (peaks, totals, accums)


def on_device(context_queries, context_keys, context_values, doc_ids, query_token_rows, span_start):
    factor = float(HEAD_SIZE) ** (-0.5)
    host_index = lax.axis_index("hosts")
    host_count = lax.axis_size("hosts")
    block_len = context_queries.shape[0]
    per_host = query_token_rows.shape[0]
    stacked = jnp.stack([context_keys, context_values])
    anchor = from_root(stacked, "hosts", 0)
    key_rows = jnp.concatenate([anchor[0], context_keys], 0)
    value_rows = jnp.concatenate([anchor[1], context_values], 0)
    positions = jnp.arange(block_len, dtype=jnp.int32)
    causal = positions[None, :] <= positions[:, None]
    own_visible = causal & (doc_ids[:, None] == doc_ids[None, :])
    front_visible = jnp.broadcast_to(host_index > 0, (block_len, block_len))
    visible = jnp.concatenate([front_visible, own_visible], 1)
    block_out = block_attention(context_queries, key_rows, value_rows, visible, factor)
    all_queries, all_spans = (
        lax.all_gather(query_token_rows, "hosts", axis=0, tiled=True),
        lax.all_gather(span_start, "hosts", axis=0, tiled=True),
    )
    key_positions = host_index * block_len + positions
    query_visible = key_positions[None, :] >= all_spans[:, None]
    peaks, totals, accums = query_partials(
        all_queries, context_keys, context_values, query_visible, factor
    )
    received = (
        lax.all_to_all(peaks, "hosts", split_axis=0, concat_axis=0, tiled=True),
        lax.all_to_all(totals, "hosts", split_axis=0, concat_axis=0, tiled=True),
        lax.all_to_all(accums, "hosts", split_axis=0, concat_axis=0, tiled=True),
    )
    source_peaks = received[0].reshape(host_count, per_host, -1)
    source_totals = received[1].reshape(host_count, per_host, -1)
    source_accums = received[2].reshape(host_count, per_host, -1)
    overall = jnp.max(source_peaks, 0)
    scales = jnp.exp(source_peaks - overall[None])
    own_totals = jnp.sum(scales * source_totals, 0)
    own_accums = jnp.sum(jnp.repeat(scales, HEAD_SIZE, axis=2) * source_accums, 0)
    answer = (own_accums / jnp.repeat(own_totals, HEAD_SIZE, axis=1)).astype(jnp.bfloat16)
    return (block_out, answer)


def solution(mesh):
    in_specs = (
        P(("groups", "hosts"), "tensor"),
        P(("groups", "hosts"), "tensor"),
        P(("groups", "hosts"), "tensor"),
        P(("groups", "hosts")),
        P(("groups", "hosts"), "tensor"),
        P(("groups", "hosts")),
    )
    out_specs = (P(("groups", "hosts"), "tensor"), P(("groups", "hosts"), "tensor"))
    return jax.shard_map(
        on_device, mesh=mesh, in_specs=in_specs, out_specs=out_specs, check_vma=False
    )
```

profile of v0, /device:TPU:0, one launch (start us, length us, event | category | flops | bytes accessed | tf_op | source)
XLA Modules:
  0.0 166.9 jit_solution(4238791645243524496)
XLA Ops:
  7.2 0.0 copy-start.2
  7.2 1.1 copy.26
  8.9 0.0 copy-start.5
  9.0 0.6 copy-done.5
  9.6 0.6 dynamic-slice
  10.2 0.8 dynamic-update-slice
  11.0 0.1 copy.27
  11.1 13.1 %all-reduce.1 = s32[8]{0:T(128)S(1)} all-reduce(s32[8]{0:T(128)S(1)} %dynamic-update-slice), channel_id=1, replica_groups=mesh['groups'=2,'hosts'=8,'tensor'=2] {'hosts'}, use_global_device_ids=true, to_apply=%add.1 | all-reduce | flops 8 | bytes 64
  24.2 30.5 %all-gather = bf16[8,1,4096]{2,1,0:T(2,128)(2,1)S(1)} all-gather(bf16[1,1,4096]{2,1,0:T(2,128)(2,1)S(1)} %bitcast.124), channel_id=1, replica_groups=mesh['groups'=2,'hosts'=8,'tensor'=2] {'hosts'}, dimensions={0}, use_global_device_ids=true | all-gather | bytes 73728 | tf_op jit(solution)/shard_map/all_gather | solution.py:111
  54.7 0.4 reduce.5
  55.1 2.7 %while.26 = (s32[]{:T(128)}, f32[4,8,8]{2,1,0:T(8,128)S(1)}, f32[4,8,8]{2,1,0:T(8,128)S(1)}, f32[4,8,8,128]{3,2,1,0:T(8,128)S(1)}, bf16[4,8,8,128]{3,2,0,1:T(8,1...) while((s32[]{:T(128)}, f32[4,8,8]{2,1,0:T(8,128)S(1)}, ...), condition=%wide.region_8.9_spmd.clone, body=%wide.region_5.8_spmd.clone.sunk | while | flops 4268930 | bytes 241033 | solution.py:79
  55.1 0.1 broadcast_compare_fusion.2
  55.1 0.2 select_reduce_fusion.3
  55.4 0.2 fusion.74
  55.6 0.2 fusion.73
  55.8 0.1 broadcast_compare_fusion.2
  55.8 0.2 select_reduce_fusion.3
  56.0 0.2 fusion.74
  56.2 0.2 fusion.73
  56.4 0.1 broadcast_compare_fusion.2
  56.5 0.2 select_reduce_fusion.3
  56.7 0.2 fusion.74
  56.9 0.2 fusion.73
  57.1 0.1 broadcast_compare_fusion.2
  57.2 0.2 select_reduce_fusion.3
  57.4 0.2 fusion.74
  57.6 0.2 fusion.73
  57.8 0.0 copy-start
  57.8 0.7 all_to_all.18
  58.5 3.3 %all-to-all-start = ((f32[8,1,32]{2,1,0:T(1,128)}), f32[8,1,32]{2,1,0:T(1,128)S(1)}, u32[]{:S(2)}, u32[]{:S(2)}) async-start(f32[8,1,32]{2,1,0:T(1,128)} %bitcast.23), calls=%async_computation | async-start | bytes 8192 | tf_op jit(solution)/shard_map/all_to_all | solution.py:120
  61.8 0.7 all_to_all.22
  62.5 5.6 %all-to-all-done = f32[8,1,32]{2,1,0:T(1,128)S(1)} async-done(((f32[8,1,32]{2,1,0:T(1,128)}), f32[8,1,32]{2,1,0:T(1,128)S(1)}, u32[]{:S(2)}, u32[]{:S(2)}) %all-to-all-start) | async-done | bytes 1056 | tf_op jit(solution)/shard_map/all_to_all | solution.py:120
  68.1 3.3 %all-to-all-start.2 = ((f32[8,1,32]{2,1,0:T(1,128)}), f32[8,1,32]{2,1,0:T(1,128)S(1)}, u32[]{:S(2)}, u32[]{:S(2)}) async-start(f32[8,1,32]{2,1,0:T(1,128)} %bitcast.30), calls=%async_computation.2 | async-start | bytes 8192 | tf_op jit(solution)/shard_map/all_to_all | solution.py:121
  71.5 0.0 all-reduce.4.cloned.1.call-start
  71.5 0.7 maximum_select_fusion
  72.2 0.0 all-reduce.4.cloned.1.call-update
  72.3 0.7 copy.39
  72.9 4.9 %all-to-all-done.2 = f32[8,1,32]{2,1,0:T(1,128)S(1)} async-done(((f32[8,1,32]{2,1,0:T(1,128)}), f32[8,1,32]{2,1,0:T(1,128)S(1)}, u32[]{:S(2)}, u32[]{:S(2)}) %all-to-all-start.2) | async-done | bytes 1056 | tf_op jit(solution)/shard_map/all_to_all | solution.py:121
  77.8 3.5 %all-to-all-start.1 = ((f32[8,1,4096]{2,1,0:T(1,128)}), f32[8,1,4096]{2,1,0:T(1,128)S(1)}, u32[]{:S(2)}, u32[]{:S(2)}) async-start(f32[8,1,4096]{2,1,0:T(1,128)} %bitcast.27), calls=%async_computation.1 | async-start | bytes 262144 | tf_op jit(solution)/shard_map/all_to_all | solution.py:122
  81.3 0.1 fusion.50
  81.4 0.7 copy.25
  82.2 6.7 %all-to-all-done.1 = f32[8,1,4096]{2,1,0:T(1,128)S(1)} async-done(((f32[8,1,4096]{2,1,0:T(1,128)}), f32[8,1,4096]{2,1,0:T(1,128)S(1)}, u32[]{:S(2)}, u32[]{:S(2)}) %all-to-all-start.1) | async-done | bytes 131104 | tf_op jit(solution)/shard_map/all_to_all | solution.py:122
  88.9 0.1 broadcast_in_dim.87
  89.0 0.2 multiply_reduce_fusion
  89.2 0.1 broadcast_in_dim.89
  89.3 0.6 divide_convert_fusion
  89.9 58.0 %all-reduce.4.cloned.1.call-done = bf16[2,128,512]{1,2,0:T(8,128)(2,1)} async-done(((bf16[2,128,512]{1,2,0:T(8,128)(2,1)}), bf16[2,128,512]{1,2,0:T(8,128)(2,1)}) %all-reduce.4.cloned.1.call-update) | async-done | bytes 262160 | tf_op jit(solution)/shard_map/psum | solution.py:12
  147.9 1.0 fusion.52
  148.9 0.8 maximum_bitcast_fusion
  149.6 8.3 %while.25 = (s32[]{:T(128)}, bf16[4,128,8,128]{3,1,2,0:T(8,128)(2,1)S(1)}, pred[128,256]{1,0:T(8,128)(4,1)S(1)}, bf16[4,128,8,128]{1,3,2,0:T(8,128)(2,1)S(1)}, b...) while((s32[]{:T(128)}, bf16[4,128,8,128]{3,1,2,0:T(8,128)(2,1)S(1)}, ...), condition=%wide.region_4.5_spmd, body=%wide.region_1.4_spmd.sunk | while | flops 136840704 | bytes 4958285 | solution.py:47
  149.6 0.3 convolution_multiply_fusion.3
  150.0 0.4 fusion.69
  150.4 1.3 fusion.70
  151.7 0.3 convolution_multiply_fusion.3
  152.1 0.4 fusion.69
  152.5 1.3 fusion.70
  153.8 0.3 convolution_multiply_fusion.3
  154.2 0.4 fusion.69
  154.6 1.3 fusion.70
  155.9 0.3 convolution_multiply_fusion.3
  156.2 0.4 fusion.69
  156.7 1.3 fusion.70
  158.0 0.7 copy.33
  158.7 1.4 copy.53
  (24 shorter events, 0.2 us)
Async XLA Ops:
  7.2 3.7 %copy-start.2 = (bf16[128,512]{1,0:T(8,128)(2,1)S(1)}, bf16[128,512]{1,0:T(8,128)(2,1)}, u32[]{:S(2)}) copy-start(bf16[128,512]{1,0:T(8,128)(2,1)} %param.12) | copy-start | bytes 393220
  8.9 0.7 copy-start.5
  10.9 13.2 %copy-start.3 = (bf16[1,4096]{1,0:T(2,128)(2,1)S(1)}, bf16[1,4096]{1,0:T(2,128)(2,1)}, u32[]{:S(2)}) copy-start(bf16[1,4096]{1,0:T(2,128)(2,1)} %param.14) | copy-start | bytes 24580
  57.8 23.6 %copy-start = (bf16[128,4096]{1,0:T(8,128)(2,1)S(1)}, bf16[128,4096]{1,0:T(8,128)(2,1)}, u32[]{:S(2)}) copy-start(bf16[128,4096]{1,0:T(8,128)(2,1)} %param.10) | copy-start | bytes 3145732
  58.5 9.6 %all-to-all-start = ((f32[8,1,32]{2,1,0:T(1,128)}), f32[8,1,32]{2,1,0:T(1,128)S(1)}, u32[]{:S(2)}, u32[]{:S(2)}) async-start(f32[8,1,32]{2,1,0:T(1,128)} %bitcast.23), calls=%async_computation | async-start | bytes 8192 | tf_op jit(solution)/shard_map/all_to_all | solution.py:120
  68.1 9.6 %all-to-all-start.2 = ((f32[8,1,32]{2,1,0:T(1,128)}), f32[8,1,32]{2,1,0:T(1,128)S(1)}, u32[]{:S(2)}, u32[]{:S(2)}) async-start(f32[8,1,32]{2,1,0:T(1,128)} %bitcast.30), calls=%async_computation.2 | async-start | bytes 8192 | tf_op jit(solution)/shard_map/all_to_all | solution.py:121
  71.5 76.4 %all-reduce.4.cloned.1.call-start = ((), (), s32[]{:S(2)}) async-start(), calls=%async_computation.3 | async-start | bytes 524288 | tf_op jit(solution)/shard_map/psum | solution.py:12
  77.8 3.5 %copy-start.4 = (s32[128]{0:T(128)S(1)}, s32[128]{0:T(128)}, u32[]{:S(2)}) copy-start(s32[128]{0:T(128)} %param.13) | copy-start | bytes 1540
  77.8 11.1 %all-to-all-start.1 = ((f32[8,1,4096]{2,1,0:T(1,128)}), f32[8,1,4096]{2,1,0:T(1,128)S(1)}, u32[]{:S(2)}, u32[]{:S(2)}) async-start(f32[8,1,4096]{2,1,0:T(1,128)} %bitcast.27), calls=%async_computation.1 | async-start | bytes 262144 | tf_op jit(solution)/shard_map/all_to_all | solution.py:122
  82.1 67.5 %copy-start.1 = (bf16[4,128,8,128]{3,1,2,0:T(8,128)(2,1)S(1)}, bf16[4,128,8,128]{3,1,2,0:T(8,128)(2,1)}, u32[]{:S(2)}) copy-start(bf16[4,128,8,128]{3,1,2,0:T(8,128)(2,1)} %custom-call) | copy-start | bytes 3145732
Sparse Core Ops, SparseCore 0:
  75.7 72.1 all-reduce.3
where the time goes:
time: 168 us; the launch traced here: 167 us
  waiting for transfers between devices  75.3 us (45%)
  blocking collectives  43.6 us (26%)
  between operations  14.9 us (9%)
  starting transfers between devices  10.2 us (6%)
  local copies, waits for them, and re-layouts  9.16 us (5%)
  matrix products  8.18 us (5%)
  other arithmetic  5.46 us (3%)
    psum x1, waiting for transfers between devices, from_root(): return lax.psum(kept, axis)  58 us
    all_gather x1, blocking collectives, on_device(): lax.all_gather(query_token_rows, 'hosts', axis=0, tiled=True)  30.5 us
    unnamed x1, blocking collectives  13.1 us
    all_to_all x1, waiting for transfers between devices, on_device(): lax.all_to_all(accums, 'hosts', split_axis=0, concat_axis=0, tiled=True)  6.74 us
    all_to_all x1, waiting for transfers between devices, on_device(): lax.all_to_all(peaks, 'hosts', split_axis=0, concat_axis=0, tiled=True)  5.63 us
    unnamed x20, local copies, waits for them, and re-layouts  5.27 us
    dot_general x4, matrix products, block_per_head(): jnp.einsum('rgs,sd->rgd', weights.astype(jnp.bfloat16), value_part, prefe...  5.21 us
    all_to_all x1, waiting for transfers between devices, on_device(): lax.all_to_all(totals, 'hosts', split_axis=0, concat_axis=0, tiled=True)  4.86 us
  transfers between devices with their start and end apart: 4, of which 4 were waited for; matrix products, arithmetic and copies ran while one was open for 2% of the time, Pallas kernels for 0%

commit v1 on v0

--- a/solution.py
+++ b/solution.py
@@ -1,10 +1,34 @@
+import functools
 import jax
 import jax.numpy as jnp
 from jax import lax
 from jax.sharding import PartitionSpec as P
+from jax.lax import axis_index, axis_size, ppermute
 
 HEAD_SIZE = 128
 MASKED_SCORE = -1e30
+
+
+def follow_columns_here(mat, which_axis):
+    amount_of = axis_size(which_axis)
+    inbox = [(k0, (k0 + 1) % amount_of) for k0 in range(amount_of)]
+    grid = [(k0, (k0 - 1) % amount_of) for k0 in range(amount_of)]
+    z1, ready = ([mat], [mat])
+    for _ in range(amount_of // 2):
+        long_array = ppermute(z1[-1], axis_name=which_axis, perm=inbox)
+        z1.append(long_array)
+    k = 0
+    while k < (amount_of - 1) // 2:
+        current_block = ppermute(ready[-1], axis_name=which_axis, perm=grid)
+        ready.append(current_block)
+        k = k + 1
+    top = jnp.concatenate([*z1[::-1], *ready[1:]], axis=0)
+    k_now = axis_index(which_axis)
+    met_up = jnp.roll(top, (k_now - amount_of // 2) * mat.shape[0], axis=0)
+    return met_up
+
+
+part_joints = functools.partial(follow_columns_here, which_axis="hosts")
 
 
 def from_root(value, axis, source):
@@ -108,7 +132,7 @@
     visible = jnp.concatenate([front_visible, own_visible], 1)
     block_out = block_attention(context_queries, key_rows, value_rows, visible, factor)
     all_queries, all_spans = (
-        lax.all_gather(query_token_rows, "hosts", axis=0, tiled=True),
+        part_joints(query_token_rows),
         lax.all_gather(span_start, "hosts", axis=0, tiled=True),
     )
     key_positions = host_index * block_len + positions

time: 168 us -> 148 us (0.88)
  blocking collectives: 43.6 us -> 11.3 us
  starting transfers between devices: 10.2 us -> 25.6 us
  waiting for transfers between devices: 75.3 us -> 69.6 us
  local copies, waits for them, and re-layouts: 9.16 us -> 12.4 us
    all_gather x1 -> x0, blocking collectives: 30.5 us -> none  [on_device(): lax.all_gather(query_token_rows, 'hosts', axis=0, tiled=True)]
    ppermute x0 -> x7, starting transfers between devices: none -> 15.6 us  [the longest x3 12.6 us: follow_columns_here(): current_block = ppermute(ready[-1], axis_name=which_axis, perm=grid)]
    all_to_all x1, waiting for transfers between devices: 6.74 us -> 0.01 us  [on_device(): lax.all_to_all(accums, 'hosts', split_axis=0, concat_axis=0, tiled=True)]
    ppermute x0 -> x7, waiting for transfers between devices: none -> 3.53 us  [the longest x4 3.52 us: follow_columns_here(): long_array = ppermute(z1[-1], axis_name=which_axis, perm=inbox)]
    unnamed x1, blocking collectives: 13.1 us -> 11.3 us
    unnamed x20 -> x21, local copies, waits for them, and re-layouts: 5.27 us -> 5.86 us
  transfers between devices with their start and end apart: 4 -> 11, of which waited for: 4 -> 5; matrix products, arithmetic and copies ran while one was open for 2% -> 12% of each run, Pallas kernels for 0% -> 0%
where the time goes in v1:
time: 148 us
  waiting for transfers between devices  69.6 us (47%)
  starting transfers between devices  25.6 us (17%)
  between operations  14.9 us (10%)
  local copies, waits for them, and re-layouts  12.4 us (8%)
  blocking collectives  11.3 us (8%)
  matrix products  8.34 us (6%)
  other arithmetic  5.08 us (3%)
    psum x1, waiting for transfers between devices, from_root(): return lax.psum(kept, axis)  57 us
    ppermute x3, starting transfers between devices, follow_columns_here(): current_block = ppermute(ready[-1], axis_name=which_axis, perm=grid)  12.6 us
    unnamed x1, blocking collectives  11.3 us
    unnamed x21, local copies, waits for them, and re-layouts  5.86 us
    dot_general x4, matrix products, block_per_head(): jnp.einsum('rgs,sd->rgd', weights.astype(jnp.bfloat16), value_part, prefe...  5.35 us
    all_to_all x1, waiting for transfers between devices, on_device(): lax.all_to_all(peaks, 'hosts', split_axis=0, concat_axis=0, tiled=True)  4.86 us
    all_to_all x1, waiting for transfers between devices, on_device(): lax.all_to_all(totals, 'hosts', split_axis=0, concat_axis=0, tiled=True)  4.23 us
    ppermute x4, waiting for transfers between devices, follow_columns_here(): long_array = ppermute(z1[-1], axis_name=which_axis, perm=inbox)  3.52 us
  transfers between devices with their start and end apart: 11, of which 5 were waited for; matrix products, arithmetic and copies ran while one was open for 12% of the time, Pallas kernels for 0%

profile of v1, /device:TPU:0, one launch (start us, length us, event | category | flops | bytes accessed | tf_op | source)
XLA Modules:
  0.0 147.5 jit_solution(6282432589137022648)
XLA Ops:
  7.2 3.0 %collective-permute-start = (bf16[1,4096]{1,0:T(2,128)(2,1)}, bf16[1,4096]{1,0:T(2,128)(2,1)S(1)}, u32[]{:S(2)}, u32[]{:S(2)}) collective-permute-start(bf16[1,4096]{1,0:T(2,128)(2,1)} %param.14), channel_id=1, source_target_pairs={{0,2},{2,4},{4,6},{6,8},{8,10},{10,12},{12,14},{14,0},{1,3},{3,5},... | collective-permute-start | bytes 24584 | tf_op jit(solution)/shard_map/ppermute | solution.py:18
  10.2 3.1 %collective-permute-start.4 = (bf16[1,4096]{1,0:T(2,128)(2,1)}, bf16[1,4096]{1,0:T(2,128)(2,1)S(1)}, u32[]{:S(2)}, u32[]{:S(2)}) collective-permute-start(bf16[1,4096]{1,0:T(2,128)(2,1)} %param.14), channel_id=1, source_target_pairs={{0,14},{2,0},{4,2},{6,4},{8,6},{10,8},{12,10},{14,12},{1,15},{3,1}... | collective-permute-start | bytes 24584 | tf_op jit(solution)/shard_map/ppermute | solution.py:22
  13.3 1.9 %collective-permute-done = bf16[1,4096]{1,0:T(2,128)(2,1)S(1)} collective-permute-done((bf16[1,4096]{1,0:T(2,128)(2,1)}, bf16[1,4096]{1,0:T(2,128)(2,1)S(1)}, u32[]{:S(2)}, u32[]{:S(2)}) %collective-permute-start) | collective-permute-done | bytes 8224 | tf_op jit(solution)/shard_map/ppermute | solution.py:18
  15.1 4.8 %collective-permute-start.5 = (bf16[1,4096]{1,0:T(2,128)(2,1)S(1)}, bf16[1,4096]{1,0:T(2,128)(2,1)S(1)}, u32[]{:S(2)}, u32[]{:S(2)}) collective-permute-start(bf16[1,4096]{1,0:T(2,128)(2,1)S(1)} %collective-permute-done.4), channel_id=1, source_target_pairs={{0,14},{2,0},{4,2},{6,4},{8,6},{10,8},{12,10},{14,12},{1,15},{3,1}... | collective-permute-start | bytes 24584 | tf_op jit(solution)/shard_map/ppermute | solution.py:22
  19.9 1.7 %collective-permute-done.1 = bf16[1,4096]{1,0:T(2,128)(2,1)S(1)} collective-permute-done((bf16[1,4096]{1,0:T(2,128)(2,1)S(1)}, bf16[1,4096]{1,0:T(2,128)(2,1)S(1)}, u32[]{:S(2)}, u32[]{:S(2)}) %collective-permute-start.1) | collective-permute-done | bytes 8224 | tf_op jit(solution)/shard_map/ppermute | solution.py:18
  22.2 0.6 copy-done.6
  22.9 0.6 dynamic-slice
  23.5 0.8 dynamic-update-slice
  24.2 4.7 %collective-permute-start.6 = (bf16[1,4096]{1,0:T(2,128)(2,1)S(1)}, bf16[1,4096]{1,0:T(2,128)(2,1)S(1)}, u32[]{:S(2)}, u32[]{:S(2)}) collective-permute-start(bf16[1,4096]{1,0:T(2,128)(2,1)S(1)} %collective-permute-done.5), channel_id=1, source_target_pairs={{0,14},{2,0},{4,2},{6,4},{8,6},{10,8},{12,10},{14,12},{1,15},{3,1}... | collective-permute-start | bytes 24584 | tf_op jit(solution)/shard_map/ppermute | solution.py:22
  29.0 11.3 %all-reduce.1 = s32[8]{0:T(128)S(1)} all-reduce(s32[8]{0:T(128)S(1)} %dynamic-update-slice), channel_id=1, replica_groups=mesh['groups'=2,'hosts'=8,'tensor'=2] {'hosts'}, use_global_device_ids=true, to_apply=%add.1 | all-reduce | flops 8 | bytes 64
  40.3 1.1 copy.26
  41.3 0.1 copy.27
  41.5 0.6 copy-done.3
  42.0 0.4 concatenate.32
  42.5 2.7 %while.26 = (s32[]{:T(128)}, f32[4,8,8]{2,1,0:T(8,128)S(1)}, f32[4,8,8]{2,1,0:T(8,128)S(1)}, f32[4,8,8,128]{3,2,1,0:T(8,128)S(1)}, bf16[4,8,8,128]{3,2,0,1:T(8,1...) while((s32[]{:T(128)}, f32[4,8,8]{2,1,0:T(8,128)S(1)}, ...), condition=%wide.region_8.9_spmd.clone, body=%wide.region_5.8_spmd.clone.sunk | while | flops 4268930 | bytes 241033 | solution.py:103
  42.6 0.2 select_reduce_fusion.3
  42.8 0.2 fusion.74
  43.0 0.2 fusion.73
  43.3 0.2 select_reduce_fusion.3
  43.5 0.2 fusion.74
  43.7 0.2 fusion.73
  44.0 0.2 select_reduce_fusion.3
  44.2 0.2 fusion.74
  44.4 0.2 fusion.73
  44.7 0.2 select_reduce_fusion.3
  44.9 0.2 fusion.74
  45.1 0.2 fusion.73
  45.3 0.7 all_to_all.18
  45.9 3.3 %all-to-all-start = ((f32[8,1,32]{2,1,0:T(1,128)}), f32[8,1,32]{2,1,0:T(1,128)S(1)}, u32[]{:S(2)}, u32[]{:S(2)}) async-start(f32[8,1,32]{2,1,0:T(1,128)} %bitcast.22), calls=%async_computation | async-start | bytes 8192 | tf_op jit(solution)/shard_map/all_to_all | solution.py:144
  49.3 0.7 maximum_select_fusion
  50.1 0.7 all_to_all.22
  50.8 4.9 %all-to-all-done = f32[8,1,32]{2,1,0:T(1,128)S(1)} async-done(((f32[8,1,32]{2,1,0:T(1,128)}), f32[8,1,32]{2,1,0:T(1,128)S(1)}, u32[]{:S(2)}, u32[]{:S(2)}) %all-to-all-start) | async-done | bytes 1056 | tf_op jit(solution)/shard_map/all_to_all | solution.py:144
  55.6 3.3 %all-to-all-start.2 = ((f32[8,1,32]{2,1,0:T(1,128)}), f32[8,1,32]{2,1,0:T(1,128)S(1)}, u32[]{:S(2)}, u32[]{:S(2)}) async-start(f32[8,1,32]{2,1,0:T(1,128)} %bitcast.29), calls=%async_computation.2 | async-start | bytes 8192 | tf_op jit(solution)/shard_map/all_to_all | solution.py:145
  59.0 0.1 fusion.50
  59.1 0.7 copy.25
  59.7 0.6 concatenate.25
  60.4 0.7 copy.39
  61.0 4.2 %all-to-all-done.2 = f32[8,1,32]{2,1,0:T(1,128)S(1)} async-done(((f32[8,1,32]{2,1,0:T(1,128)}), f32[8,1,32]{2,1,0:T(1,128)S(1)}, u32[]{:S(2)}, u32[]{:S(2)}) %all-to-all-start.2) | async-done | bytes 1056 | tf_op jit(solution)/shard_map/all_to_all | solution.py:145
  65.3 3.4 %all-to-all-start.1 = ((f32[8,1,4096]{2,1,0:T(1,128)}), f32[8,1,4096]{2,1,0:T(1,128)S(1)}, u32[]{:S(2)}, u32[]{:S(2)}) async-start(f32[8,1,4096]{2,1,0:T(1,128)} %bitcast.26), calls=%async_computation.1 | async-start | bytes 262144 | tf_op jit(solution)/shard_map/all_to_all | solution.py:146
  68.7 57.0 %all-reduce.4.cloned.1.call-done = bf16[2,128,512]{1,2,0:T(8,128)(2,1)} async-done(((bf16[2,128,512]{1,2,0:T(8,128)(2,1)}), bf16[2,128,512]{1,2,0:T(8,128)(2,1)}) %all-reduce.4.cloned.1.call-update) | async-done | bytes 262160 | tf_op jit(solution)/shard_map/psum | solution.py:36
  125.7 1.0 fusion.52
  126.7 0.8 maximum_bitcast_fusion
  127.4 10.2 %while.25 = (s32[]{:T(128)}, bf16[4,128,8,128]{3,1,2,0:T(8,128)(2,1)S(1)}, pred[128,256]{1,0:T(8,128)(4,1)}, bf16[4,128,8,128]{1,3,2,0:T(8,128)(2,1)S(1)}, bf16[...) while((s32[]{:T(128)}, bf16[4,128,8,128]{3,1,2,0:T(8,128)(2,1)S(1)}, ...), condition=%wide.region_4.5_spmd, body=%wide.region_1.4_spmd.sunk | while | flops 136840704 | bytes 5089385 | solution.py:71
  127.4 0.3 convolution_multiply_fusion.3
  127.8 0.4 copy-done.4
  128.2 0.4 fusion.69
  128.6 1.3 fusion.70
  130.0 0.3 convolution_multiply_fusion.3
  130.3 0.4 copy-done.4
  130.7 0.4 fusion.69
  131.2 1.3 fusion.70
  132.5 0.3 convolution_multiply_fusion.3
  132.9 0.4 copy-done.4
  133.3 0.4 fusion.69
  133.7 1.3 fusion.70
  135.1 0.3 convolution_multiply_fusion.3
  135.4 0.4 copy-done.4
  135.8 0.4 fusion.69
  136.3 1.3 fusion.70
  137.6 0.7 copy.33
  138.3 1.4 copy.53
  139.7 0.1 broadcast_in_dim.87
  139.8 0.2 multiply_reduce_fusion
  140.1 0.6 divide_convert_fusion
  (46 shorter events, 0.6 us)
Async XLA Ops:
  7.2 8.0 %collective-permute-start = (bf16[1,4096]{1,0:T(2,128)(2,1)}, bf16[1,4096]{1,0:T(2,128)(2,1)S(1)}, u32[]{:S(2)}, u32[]{:S(2)}) collective-permute-start(bf16[1,4096]{1,0:T(2,128)(2,1)} %param.14), channel_id=1, source_target_pairs={{0,2},{2,4},{4,6},{6,8},{8,10},{10,12},{12,14},{14,0},{1,3},{3,5},... | collective-permute-start | bytes 24584 | tf_op jit(solution)/shard_map/ppermute | solution.py:18
  10.2 5.0 %collective-permute-start.4 = (bf16[1,4096]{1,0:T(2,128)(2,1)}, bf16[1,4096]{1,0:T(2,128)(2,1)S(1)}, u32[]{:S(2)}, u32[]{:S(2)}) collective-permute-start(bf16[1,4096]{1,0:T(2,128)(2,1)} %param.14), channel_id=1, source_target_pairs={{0,14},{2,0},{4,2},{6,4},{8,6},{10,8},{12,10},{14,12},{1,15},{3,1}... | collective-permute-start | bytes 24584 | tf_op jit(solution)/shard_map/ppermute | solution.py:22
  15.1 6.4 %collective-permute-start.1 = (bf16[1,4096]{1,0:T(2,128)(2,1)S(1)}, bf16[1,4096]{1,0:T(2,128)(2,1)S(1)}, u32[]{:S(2)}, u32[]{:S(2)}) collective-permute-start(bf16[1,4096]{1,0:T(2,128)(2,1)S(1)} %collective-permute-done), channel_id=1, source_target_pairs={{0,2},{2,4},{4,6},{6,8},{8,10},{10,12},{12,14},{14,0},{1,3},{3,5},... | collective-permute-start | bytes 24584 | tf_op jit(solution)/shard_map/ppermute | solution.py:18
  15.1 9.1 %collective-permute-start.5 = (bf16[1,4096]{1,0:T(2,128)(2,1)S(1)}, bf16[1,4096]{1,0:T(2,128)(2,1)S(1)}, u32[]{:S(2)}, u32[]{:S(2)}) collective-permute-start(bf16[1,4096]{1,0:T(2,128)(2,1)S(1)} %collective-permute-done.4), channel_id=1, source_target_pairs={{0,14},{2,0},{4,2},{6,4},{8,6},{10,8},{12,10},{14,12},{1,15},{3,1}... | collective-permute-start | bytes 24584 | tf_op jit(solution)/shard_map/ppermute | solution.py:22
  21.6 7.4 %collective-permute-start.2 = (bf16[1,4096]{1,0:T(2,128)(2,1)S(1)}, bf16[1,4096]{1,0:T(2,128)(2,1)S(1)}, u32[]{:S(2)}, u32[]{:S(2)}) collective-permute-start(bf16[1,4096]{1,0:T(2,128)(2,1)S(1)} %collective-permute-done.1), channel_id=1, source_target_pairs={{0,2},{2,4},{4,6},{6,8},{8,10},{10,12},{12,14},{14,0},{1,3},{3,5},... | collective-permute-start | bytes 24584 | tf_op jit(solution)/shard_map/ppermute | solution.py:18
  22.2 0.7 copy-start.6
  24.2 17.3 %collective-permute-start.6 = (bf16[1,4096]{1,0:T(2,128)(2,1)S(1)}, bf16[1,4096]{1,0:T(2,128)(2,1)S(1)}, u32[]{:S(2)}, u32[]{:S(2)}) collective-permute-start(bf16[1,4096]{1,0:T(2,128)(2,1)S(1)} %collective-permute-done.5), channel_id=1, source_target_pairs={{0,14},{2,0},{4,2},{6,4},{8,6},{10,8},{12,10},{14,12},{1,15},{3,1}... | collective-permute-start | bytes 24584 | tf_op jit(solution)/shard_map/ppermute | solution.py:22
  29.0 12.5 %collective-permute-start.3 = (bf16[1,4096]{1,0:T(2,128)(2,1)S(1)}, bf16[1,4096]{1,0:T(2,128)(2,1)S(1)}, u32[]{:S(2)}, u32[]{:S(2)}) collective-permute-start(bf16[1,4096]{1,0:T(2,128)(2,1)S(1)} %collective-permute-done.2), channel_id=1, source_target_pairs={{0,2},{2,4},{4,6},{6,8},{8,10},{10,12},{12,14},{14,0},{1,3},{3,5},... | collective-permute-start | bytes 24584 | tf_op jit(solution)/shard_map/ppermute | solution.py:18
  40.3 1.1 copy-start.2
  41.3 0.7 copy-start.3
  42.5 16.6 %copy-start = (bf16[128,4096]{1,0:T(8,128)(2,1)S(1)}, bf16[128,4096]{1,0:T(8,128)(2,1)}, u32[]{:S(2)}) copy-start(bf16[128,4096]{1,0:T(8,128)(2,1)} %param.10) | copy-start | bytes 3145732
  45.9 9.7 %all-to-all-start = ((f32[8,1,32]{2,1,0:T(1,128)}), f32[8,1,32]{2,1,0:T(1,128)S(1)}, u32[]{:S(2)}, u32[]{:S(2)}) async-start(f32[8,1,32]{2,1,0:T(1,128)} %bitcast.22), calls=%async_computation | async-start | bytes 8192 | tf_op jit(solution)/shard_map/all_to_all | solution.py:144
  49.3 76.4 %all-reduce.4.cloned.1.call-start = ((), (), s32[]{:S(2)}) async-start(), calls=%async_computation.3 | async-start | bytes 524288 | tf_op jit(solution)/shard_map/psum | solution.py:36
  50.1 8.9 %copy-start.5 = (s32[128]{0:T(128)S(1)}, s32[128]{0:T(128)}, u32[]{:S(2)}) copy-start(s32[128]{0:T(128)} %param.13) | copy-start | bytes 1540
  55.6 9.6 %all-to-all-start.2 = ((f32[8,1,32]{2,1,0:T(1,128)}), f32[8,1,32]{2,1,0:T(1,128)S(1)}, u32[]{:S(2)}, u32[]{:S(2)}) async-start(f32[8,1,32]{2,1,0:T(1,128)} %bitcast.29), calls=%async_computation.2 | async-start | bytes 8192 | tf_op jit(solution)/shard_map/all_to_all | solution.py:145
  60.4 67.1 %copy-start.1 = (bf16[4,128,8,128]{3,1,2,0:T(8,128)(2,1)S(1)}, bf16[4,128,8,128]{3,1,2,0:T(8,128)(2,1)}, u32[]{:S(2)}) copy-start(bf16[4,128,8,128]{3,1,2,0:T(8,128)(2,1)} %custom-call) | copy-start | bytes 3145732
  65.3 74.5 %all-to-all-start.1 = ((f32[8,1,4096]{2,1,0:T(1,128)}), f32[8,1,4096]{2,1,0:T(1,128)S(1)}, u32[]{:S(2)}, u32[]{:S(2)}) async-start(f32[8,1,4096]{2,1,0:T(1,128)} %bitcast.26), calls=%async_computation.1 | async-start | bytes 262144 | tf_op jit(solution)/shard_map/all_to_all | solution.py:146
  127.4 0.8 copy-start.4
  130.0 0.8 copy-start.4
  132.5 0.8 copy-start.4
  135.1 0.8 copy-start.4
Sparse Core Ops, SparseCore 0:
  53.5 72.1 all-reduce.3
